TPU v7x, 32 devices: a whole 2x2x4 slice. The times are simulated.
32 devices in a mesh: real: 2 (over y), slab: 4 (over z), pencil: 2 (over x), sub: 2 (over core).
Axes of the slice: x: 2, y: 2, z: 4, core: 2. Of those that a mesh axis runs over, the one named last changes fastest.
Arguments:
- permeability: float32 [128, 64, 256], P(('real', 'slab'), ('pencil', 'sub')), parts along dimension 0, may hold values from 0.1 to 10
- source: float32 [128, 64, 256], P(('real', 'slab'), ('pencil', 'sub')), parts along dimension 0, may hold values from -24 to 24
- pressure: float32 [128, 64, 256], P(('real', 'slab'), ('pencil', 'sub')), parts along dimension 0, may hold values from -24 to 24
- aggregate: int32 [128], P('real'), parts along dimension 0, may hold values from 0 to 31, as said below
Outputs:
- pressure_out: float32 [128, 64, 256], P(('real', 'slab'), ('pencil', 'sub')), parts along dimension 0
There are 2 independent parts, one for each index of `real`. A program takes and returns all parts, laid end to end along the dimension named above; each array names one. Nothing has to cross between parts.
Inputs may be any that keep to these rules, and one draw needn't show every extreme that they name: `aggregate`: never falls along its dimension; each value covers 1 to 4 consecutive positions, some value exactly 4; positions k * 16 - 1 and k * 16 always hold the same value.
All inputs are finite; a program needn't handle non-finite values.
Results may differ from a plain program's by a relative error of at most 0.000068.
Values sent between devices are 32-bit elements; how exact they have to be, the bound alone decides.
A program may use at most 64 MiB of HBM per device.

v0:
```python
import jax
import jax.numpy as jnp
from jax import lax
from jax.sharding import PartitionSpec as P

NU = 2
NCS = 4


OMEGA = 0.8


def padded(array, sides, width):
    for axis, dim in sides:
        count, length = (lax.axis_size(axis), array.shape[dim])
        up = [(i, (i + 1) % count) for i in range(count - 1)]
        down = [(j, i) for i, j in up]
        last = lax.slice_in_dim(array, length - width, length, axis=dim)
        leading = lax.slice_in_dim(array, 0, width, axis=dim)
        before = lax.ppermute(last, axis, up)
        after = lax.ppermute(leading, axis, down)
        array = jnp.concatenate([before, array, after], axis=dim)
    return array


def passed_along(array, axis, by):
    count = lax.axis_size(axis)
    pairs = [(i, i + by) for i in range(count) if 0 <= i + by < count]
    return lax.ppermute(array, axis, pairs)


def harmonic(lower_k, upper_k, inside):
    denom_sum = jnp.where(inside, lower_k + upper_k, 1.0)
    return jnp.where(inside, 2.0 * lower_k * upper_k / denom_sum, 0.0)


def geometry(perm_ext, glob_x, glob_y, inside_x, inside_y, total_x, total_y):
    count_z = perm_ext.shape[2]
    both_x = (inside_x[:-1] & inside_x[1:])[:, None, None] & inside_y[None, :, None]
    both_y = (inside_y[:-1] & inside_y[1:])[None, :, None] & inside_x[:, None, None]
    plane_in = inside_x[:, None, None] & inside_y[None, :, None]
    face_x = harmonic(perm_ext[:-1], perm_ext[1:], both_x)
    face_y = harmonic(perm_ext[:, :-1], perm_ext[:, 1:], both_y)
    face_z = harmonic(perm_ext[:, :, :-1], perm_ext[:, :, 1:], plane_in)
    cell_perm = perm_ext[1:-1, 1:-1]
    face_west = face_x[:-1, 1:-1]
    face_east = face_x[1:, 1:-1]
    face_south = face_y[1:-1, :-1]
    face_north = face_y[1:-1, 1:]
    zero_plane = jnp.zeros_like(cell_perm[:, :, :1])
    face_below = jnp.concatenate([zero_plane, face_z[1:-1, 1:-1]], axis=2)
    face_above = jnp.concatenate([face_z[1:-1, 1:-1], zero_plane], axis=2)
    cell_x = glob_x[1:-1]
    cell_y = glob_y[1:-1]
    index_z = jnp.arange(count_z)
    ends_x = (cell_x == 0).astype(jnp.float32) + (cell_x == total_x - 1).astype(jnp.float32)
    ends_y = (cell_y == 0).astype(jnp.float32) + (cell_y == total_y - 1).astype(jnp.float32)
    ends_z = (index_z == 0).astype(jnp.float32) + (index_z == count_z - 1).astype(jnp.float32)
    edges = ends_x[:, None, None] + ends_y[None, :, None] + ends_z[None, None, :]
    boundary = 2.0 * cell_perm * edges
    diagonal = face_west + face_east + face_south + face_north + face_below + face_above + boundary
    cell_in = plane_in[1:-1, 1:-1]
    safe_diag = jnp.where(cell_in, diagonal, 1.0)
    return (
        face_west,
        face_east,
        face_south,
        face_north,
        face_below,
        face_above,
        boundary,
        safe_diag,
    )


def apply_fine(ext_field, faces_now):
    face_west, face_east, face_south, face_north, face_below, face_above, boundary, safe_diag = (
        faces_now
    )
    center = ext_field[1:-1, 1:-1]
    zero_plane = jnp.zeros_like(center[:, :, :1])
    below_vals = jnp.concatenate([zero_plane, center[:, :, :-1]], axis=2)
    above_vals = jnp.concatenate([center[:, :, 1:], zero_plane], axis=2)
    beside_all = face_west * ext_field[:-2, 1:-1] + face_east * ext_field[2:, 1:-1]
    beside_all = beside_all + face_south * ext_field[1:-1, :-2] + face_north * ext_field[1:-1, 2:]
    beside_all = beside_all + face_below * below_vals + face_above * above_vals
    return (center, safe_diag * center - beside_all)


def fine_halo(field_in):
    return padded(field_in, (("slab", 0), (("pencil", "sub"), 1)), 1)


def body(permeability, source, pressure, aggregate):
    width_x, width_y, depth_cells = permeability.shape
    slab_index = lax.axis_index("slab")
    slab_count = lax.axis_size("slab")
    row_index = lax.axis_index(("pencil", "sub"))
    row_count = lax.axis_size(("pencil", "sub"))
    total_x = width_x * slab_count
    total_y = width_y * row_count
    fine_rim = 1
    perm_ext = padded(permeability, (("slab", 0), (("pencil", "sub"), 1)), fine_rim)
    glob_x = slab_index * width_x - fine_rim + jnp.arange(width_x + 2 * fine_rim)
    glob_y = row_index * width_y - fine_rim + jnp.arange(width_y + 2 * fine_rim)
    inside_x = (glob_x >= 0) & (glob_x < total_x)
    inside_y = (glob_y >= 0) & (glob_y < total_y)
    faces_full = geometry(perm_ext, glob_x, glob_y, inside_x, inside_y, total_x, total_y)
    faces_zero = tuple((member for member in faces_full))

    def smooth(field_in):
        for sweep_index in range(NU):
            center, product = apply_fine(fine_halo(field_in), faces_zero)
            field_in = center + OMEGA * (source - product) / faces_zero[7]
        return field_in

    pressure = smooth(pressure)
    center, product = apply_fine(fine_halo(pressure), faces_zero)
    residual = source - product
    half_y = width_y // 2
    half_z = depth_cells // 2

    def pair_sum(block_in):
        return block_in.reshape(width_x, half_y, 2, half_z, 2).sum(axis=(2, 4))

    padded_ids = jnp.concatenate([aggregate[:1], aggregate, aggregate[-1:]])
    ext_ids = lax.dynamic_slice_in_dim(padded_ids, slab_index * width_x, width_x + 2)
    local_ids = ext_ids[1:-1]
    straddles = (slab_index > 0) & (ext_ids[0] == local_ids[0])
    first_id = local_ids[0] + straddles.astype(jnp.int32)
    count_live = local_ids[-1] - first_id + 1
    slot_ids = local_ids - first_id
    crossing = (local_ids != ext_ids[2:]).astype(jnp.float32)
    face_east = faces_zero[1]
    face_north = faces_zero[3]
    face_above = faces_zero[5]
    boundary = faces_zero[6]
    east_part = pair_sum(face_east * crossing[:, None, None])
    north_part = face_north[:, 1::2].reshape(width_x, half_y, half_z, 2).sum(axis=3)
    above_part = face_above[:, :, 1::2].reshape(width_x, half_y, 2, half_z).sum(axis=2)
    stacked = jnp.stack([pair_sum(residual), east_part, north_part, above_part, pair_sum(boundary)])
    slot_range = jnp.arange(width_x)
    owner_map = (slot_ids[:, None] == slot_range[None, :]).astype(jnp.float32)
    spill_map = (slot_ids == -1).astype(jnp.float32)
    coarse = jnp.einsum("qxjk,xs->qsjk", stacked, owner_map, precision=lax.Precision.HIGHEST)
    edge_sums = jnp.einsum("qxjk,x->qjk", stacked, spill_map, precision=lax.Precision.HIGHEST)
    arriving = passed_along(edge_sums, "slab", -1)
    last_slot = (slot_range == count_live - 1).astype(jnp.float32)
    coarse = coarse + arriving[:, None] * last_slot[None, :, None, None]

    def coarse_extend(coarse_block, rim_width):
        tail_planes = lax.dynamic_slice_in_dim(
            coarse_block, count_live - rim_width, rim_width, axis=1
        )
        sent_block = jnp.concatenate([coarse_block, tail_planes], axis=1)
        wide_block = padded(sent_block, (("slab", 1), (("pencil", "sub"), 2)), rim_width)
        ahead_planes = wide_block[:, width_x + 2 * rim_width :]
        base_block = wide_block[:, : width_x + 2 * rim_width]
        return lax.dynamic_update_slice_in_dim(
            base_block, ahead_planes, rim_width + count_live, axis=1
        )

    coarse_rim = NCS
    coef_ext = coarse_extend(coarse, coarse_rim)
    coarse_corr = jnp.zeros((width_x + 2 * NCS, half_y + 2 * NCS, half_z), jnp.float32)
    for sweep_index in range(NCS):
        out_rim = NCS - 1 - sweep_index
        start_at = coarse_rim - out_rim
        size_x = width_x + 2 * out_rim
        size_y = half_y + 2 * out_rim

        def region(offset_x, offset_y):
            return coef_ext[
                :,
                start_at + offset_x : start_at + offset_x + size_x,
                start_at + offset_y : start_at + offset_y + size_y,
            ]

        here_coef = region(0, 0)
        coarse_rhs = here_coef[0]
        coarse_east = here_coef[1]
        coarse_north = here_coef[2]
        coarse_above = here_coef[3]
        coarse_bound = here_coef[4]
        coarse_west = region(-1, 0)[1]
        coarse_south = region(0, -1)[2]
        zero_plane = jnp.zeros_like(coarse_above[:, :, :1])
        coarse_below = jnp.concatenate([zero_plane, coarse_above[:, :, :-1]], axis=2)
        diag_coarse = (
            coarse_east
            + coarse_west
            + coarse_north
            + coarse_south
            + coarse_above
            + coarse_below
            + coarse_bound
        )
        safe_coarse = jnp.where(diag_coarse > 0, diag_coarse, 1.0)
        coarse_center = coarse_corr[1:-1, 1:-1]
        above_vals = jnp.concatenate([coarse_center[:, :, 1:], zero_plane], axis=2)
        below_vals = jnp.concatenate([zero_plane, coarse_center[:, :, :-1]], axis=2)
        beside_all = coarse_east * coarse_corr[2:, 1:-1] + coarse_west * coarse_corr[:-2, 1:-1]
        beside_all = (
            beside_all
            + coarse_north * coarse_corr[1:-1, 2:]
            + coarse_south * coarse_corr[1:-1, :-2]
        )
        beside_all = beside_all + coarse_above * above_vals + coarse_below * below_vals
        coarse_corr = (
            coarse_center
            + OMEGA * (coarse_rhs - (diag_coarse * coarse_center - beside_all)) / safe_coarse
        )
    corr_wide = coarse_extend(coarse_corr[None], 1)[0][:, 1:-1]
    pick_map = ((slot_ids + 1)[:, None] == jnp.arange(width_x + 2)[None, :]).astype(jnp.float32)
    correction = jnp.einsum("xs,sjk->xjk", pick_map, corr_wide, precision=lax.Precision.HIGHEST)
    correction = jnp.repeat(jnp.repeat(correction, 2, axis=1), 2, axis=2)
    pressure = pressure + correction
    return smooth(pressure)


def solution(mesh):
    in_specs = (
        P(("real", "slab"), ("pencil", "sub"), None),
        P(("real", "slab"), ("pencil", "sub"), None),
        P(("real", "slab"), ("pencil", "sub"), None),
        P("real"),
    )
    out_specs = P(("real", "slab"), ("pencil", "sub"), None)
    return jax.shard_map(body, mesh=mesh, in_specs=in_specs, out_specs=out_specs, check_vma=False)
```

profile of v0, /device:TPU:0, one launch (start us, length us, event | category | flops | bytes accessed | tf_op | source)
XLA Modules:
  0.0 179.3 jit_solution(6753484500826297644)
XLA Ops:
  2.1 5.6 %collective-permute-start.4 = (f32[1,16,256]{2,0,1:T(1,128)S(1)}, f32[1,16,256]{2,0,1:T(1,128)S(1)}, u32[]{:S(2)}, u32[]{:S(2)}) collective-permute-start(f32[1,16,256]{2,0,1:T(1,128)S(1)} %copy.61), channel_id=1, source_target_pairs={{0,4},{4,8},{8,12},{1,5},{5,9},{9,13},{2,6},{6,10},{10,14},{3,7},{... | collective-permute-start | bytes 49160 | tf_op jit(solution)/shard_map/ppermute | solution.py:20
  9.8 4.6 %collective-permute-start = (f32[1,16,256]{2,0,1:T(1,128)S(1)}, f32[1,16,256]{2,0,1:T(1,128)S(1)}, u32[]{:S(2)}, u32[]{:S(2)}) collective-permute-start(f32[1,16,256]{2,0,1:T(1,128)S(1)} %copy.56), channel_id=1, source_target_pairs={{0,4},{4,8},{8,12},{1,5},{5,9},{9,13},{2,6},{6,10},{10,14},{3,7},{... | collective-permute-start | bytes 49160 | tf_op jit(solution)/shard_map/ppermute | solution.py:20
  26.1 5.2 %collective-permute-start.6 = (f32[18,1,256]{2,0,1:T(8,128)S(1)}, f32[18,1,256]{2,0,1:T(8,128)S(1)}, u32[]{:S(2)}, u32[]{:S(2)}) collective-permute-start(f32[18,1,256]{2,0,1:T(8,128)S(1)} %get-tuple-element.25), channel_id=1, source_target_pairs={{0,1},{1,2},{2,3},{4,5},{5,6},{6,7},{8,9},{9,10},{10,11},{12,13},{... | collective-permute-start | bytes 55304 | tf_op jit(solution)/shard_map/ppermute | solution.py:20
  37.3 3.5 %collective-permute-start.8 = (f32[1,16,256]{2,0,1:T(1,128)S(1)}, f32[1,16,256]{2,0,1:T(1,128)S(1)}, u32[]{:S(2)}, u32[]{:S(2)}) collective-permute-start(f32[1,16,256]{2,0,1:T(1,128)S(1)} %get-tuple-element.41), channel_id=1, source_target_pairs={{0,4},{4,8},{8,12},{1,5},{5,9},{9,13},{2,6},{6,10},{10,14},{3,7},{... | collective-permute-start | bytes 49160 | tf_op jit(solution)/shard_map/ppermute | solution.py:20
  42.7 3.8 %collective-permute-done.9 = f32[1,16,256]{2,0,1:T(1,128)S(1)} collective-permute-done((f32[1,16,256]{2,0,1:T(1,128)S(1)}, f32[1,16,256]{2,0,1:T(1,128)S(1)}, u32[]{:S(2)}, u32[]{:S(2)}) %collective-permute-start.9) | collective-permute-done | bytes 16416 | tf_op jit(solution)/shard_map/ppermute | solution.py:21
  47.1 3.0 %collective-permute-start.10 = (f32[18,1,256]{2,0,1:T(8,128)}, f32[18,1,256]{2,0,1:T(8,128)S(1)}, u32[]{:S(2)}, u32[]{:S(2)}) collective-permute-start(f32[18,1,256]{2,0,1:T(8,128)} %get-tuple-element.21), channel_id=1, source_target_pairs={{0,1},{1,2},{2,3},{4,5},{5,6},{6,7},{8,9},{9,10},{10,11},{12,13},{... | collective-permute-start | bytes 55304 | tf_op jit(solution)/shard_map/ppermute | solution.py:20
  52.4 4.5 %slice.560 = f32[16,16,128]{2,0,1:T(8,128)S(1)} slice(f32[16,16,256]{2,0,1:T(8,128)S(1)} %concatenate.178), slice={[0:16:1], [0:16:1], [1:256:2]} | slice | bytes 262144 | tf_op jit(solution)/shard_map/slice | solution.py:140
  58.6 3.6 %collective-permute-start.12 = (f32[1,16,256]{2,0,1:T(1,128)S(1)}, f32[1,16,256]{2,0,1:T(1,128)S(1)}, u32[]{:S(2)}, u32[]{:S(2)}) collective-permute-start(f32[1,16,256]{2,0,1:T(1,128)S(1)} %get-tuple-element.37), channel_id=1, source_target_pairs={{0,4},{4,8},{8,12},{1,5},{5,9},{9,13},{2,6},{6,10},{10,14},{3,7},{... | collective-permute-start | bytes 49160 | tf_op jit(solution)/shard_map/ppermute | solution.py:20
  67.7 3.4 %reduce_sum.46 = f32[16,8,128]{0,2,1:T(8,128)S(1)} reduce(f32[16,8,2,128,2]{0,4,3,2,1:T(2,128)} %bitcast.185, f32[]{:T(128)} %constant.31.clone.1), dimensions={2,4}, to_apply=%region_1.2 | reduce | flops 49152 | bytes 327684 | tf_op jit(solution)/shard_map/reduce_sum | solution.py:124
  71.3 3.5 %reduce_sum.49 = f32[16,8,128]{0,2,1:T(8,128)S(1)} reduce(f32[16,8,2,128,2]{0,4,3,2,1:T(2,128)} %bitcast.183, f32[]{:T(128)} %constant.31.clone.1), dimensions={2,4}, to_apply=%region_4.5 | reduce | flops 49152 | bytes 327684 | tf_op jit(solution)/shard_map/reduce_sum | solution.py:124
  74.9 3.7 %collective-permute-start.14 = (f32[18,1,256]{2,0,1:T(8,128)S(1)}, f32[18,1,256]{2,0,1:T(8,128)S(1)}, u32[]{:S(2)}, u32[]{:S(2)}) collective-permute-start(f32[18,1,256]{2,0,1:T(8,128)S(1)} %get-tuple-element.19), channel_id=1, source_target_pairs={{0,1},{1,2},{2,3},{4,5},{5,6},{6,7},{8,9},{9,10},{10,11},{12,13},{... | collective-permute-start | bytes 55304 | tf_op jit(solution)/shard_map/ppermute | solution.py:20
  85.8 3.4 %reduce_sum.45 = f32[16,8,128]{0,2,1:T(8,128)S(1)} reduce(f32[16,8,2,128,2]{0,4,3,2,1:T(2,128)} %bitcast.184, f32[]{:T(128)} %constant.31.clone.1), dimensions={2,4}, to_apply=%region_0.1 | reduce | flops 49152 | bytes 327684 | tf_op jit(solution)/shard_map/reduce_sum | solution.py:124
  91.0 5.0 %collective-permute-done.16 = f32[5,8,128]{2,1,0:T(8,128)S(1)} collective-permute-done((f32[5,8,128]{2,1,0:T(8,128)S(1)}, f32[5,8,128]{2,1,0:T(8,128)S(1)}, u32[]{:S(2)}, u32[]{:S(2)}) %collective-permute-start.16) | collective-permute-done | bytes 20512 | tf_op jit(solution)/shard_map/ppermute | solution.py:29
  97.6 4.6 %collective-permute-start.17 = (f32[5,4,8,128]{3,1,2,0:T(4,128)S(1)}, f32[5,4,8,128]{3,1,2,0:T(4,128)S(1)}, u32[]{:S(2)}, u32[]{:S(2)}) collective-permute-start(f32[5,4,8,128]{3,1,2,0:T(4,128)S(1)} %get-tuple-element.13), channel_id=1, source_target_pairs={{0,4},{4,8},{8,12},{1,5},{5,9},{9,13},{2,6},{6,10},{10,14},{3,7},{... | collective-permute-start | bytes 245768 | tf_op jit(solution)/shard_map/ppermute | solution.py:20
  109.4 3.3 %collective-permute-done.20 = f32[5,28,4,128]{3,1,2,0:T(8,128)S(1)} collective-permute-done((f32[5,28,4,128]{3,1,2,0:T(8,128)S(1)}, f32[5,28,4,128]{3,1,2,0:T(8,128)S(1)}, u32[]{:S(2)}, u32[]{:S(2)}) %collective-permute-start.20) | collective-permute-done | bytes 286752 | tf_op jit(solution)/shard_map/ppermute | solution.py:21
  115.3 4.8 %dynamic_update_slice.7 = f32[5,24,16,128]{3,1,2,0:T(8,128)S(1)} dynamic-update-slice(f32[5,24,16,128]{3,1,2,0:T(8,128)S(1)} %slice.672, f32[5,4,16,128]{3,1,2,0:T(4,128)} %pad_maximum_fusion.44, s32[]{:T(128)} %constant.25.clone.1, s32[]{:T(128)S(6)} %select_n.65, s32[]{:T(128)} %constant.25.clone.1, s32[]{:T(128)} %constant.25.clone.1) | dynamic-update-slice | bytes 327684 | tf_op jit(solution)/shard_map/dynamic_update_slice | solution.py:159
  122.7 4.9 %collective-permute-start.21 = (f32[1,1,8,128]{3,1,2,0:T(1,128)S(1)}, f32[1,1,8,128]{3,1,2,0:T(1,128)S(1)}, u32[]{:S(2)}, u32[]{:S(2)}) collective-permute-start(f32[1,1,8,128]{3,1,2,0:T(1,128)S(1)} %dynamic-slice_bitcast_fusion), channel_id=1, source_target_pairs={{0,4},{4,8},{8,12},{1,5},{5,9},{9,13},{2,6},{6,10},{10,14},{3,7},{... | collective-permute-start | bytes 12296 | tf_op jit(solution)/shard_map/ppermute | solution.py:20
  129.0 6.4 %collective-permute-start.23 = (f32[1,19,1,128]{3,1,2,0:T(8,128)S(1)}, f32[1,19,1,128]{3,1,2,0:T(8,128)S(1)}, u32[]{:S(2)}, u32[]{:S(2)}) collective-permute-start(f32[1,19,1,128]{3,1,2,0:T(8,128)S(1)} %get-tuple-element.55), channel_id=1, source_target_pairs={{0,1},{1,2},{2,3},{4,5},{5,6},{6,7},{8,9},{9,10},{10,11},{12,13},{... | collective-permute-start | bytes 29192 | tf_op jit(solution)/shard_map/ppermute | solution.py:20
  143.7 4.2 %collective-permute-start.25 = (f32[1,16,256]{2,0,1:T(1,128)S(1)}, f32[1,16,256]{2,0,1:T(1,128)S(1)}, u32[]{:S(2)}, u32[]{:S(2)}) collective-permute-start(f32[1,16,256]{2,0,1:T(1,128)S(1)} %get-tuple-element.33), channel_id=1, source_target_pairs={{0,4},{4,8},{8,12},{1,5},{5,9},{9,13},{2,6},{6,10},{10,14},{3,7},{... | collective-permute-start | bytes 49160 | tf_op jit(solution)/shard_map/ppermute | solution.py:20
  149.3 4.2 %collective-permute-done.26 = f32[1,16,256]{2,0,1:T(1,128)S(1)} collective-permute-done((f32[1,16,256]{2,0,1:T(1,128)S(1)}, f32[1,16,256]{2,0,1:T(1,128)S(1)}, u32[]{:S(2)}, u32[]{:S(2)}) %collective-permute-start.26) | collective-permute-done | bytes 16416 | tf_op jit(solution)/shard_map/ppermute | solution.py:21
  153.6 3.2 %collective-permute-start.27 = (f32[18,1,256]{2,0,1:T(8,128)S(1)}, f32[18,1,256]{2,0,1:T(8,128)S(1)}, u32[]{:S(2)}, u32[]{:S(2)}) collective-permute-start(f32[18,1,256]{2,0,1:T(8,128)S(1)} %get-tuple-element.17), channel_id=1, source_target_pairs={{0,1},{1,2},{2,3},{4,5},{5,6},{6,7},{8,9},{9,10},{10,11},{12,13},{... | collective-permute-start | bytes 55304 | tf_op jit(solution)/shard_map/ppermute | solution.py:20
  161.2 3.9 %collective-permute-start.29 = (f32[1,16,256]{2,0,1:T(1,128)S(1)}, f32[1,16,256]{2,0,1:T(1,128)S(1)}, u32[]{:S(2)}, u32[]{:S(2)}) collective-permute-start(f32[1,16,256]{2,0,1:T(1,128)S(1)} %get-tuple-element.29), channel_id=1, source_target_pairs={{0,4},{4,8},{8,12},{1,5},{5,9},{9,13},{2,6},{6,10},{10,14},{3,7},{... | collective-permute-start | bytes 49160 | tf_op jit(solution)/shard_map/ppermute | solution.py:20
  166.5 4.2 %collective-permute-done.30 = f32[1,16,256]{2,0,1:T(1,128)S(1)} collective-permute-done((f32[1,16,256]{2,0,1:T(1,128)S(1)}, f32[1,16,256]{2,0,1:T(1,128)S(1)}, u32[]{:S(2)}, u32[]{:S(2)}) %collective-permute-start.30) | collective-permute-done | bytes 16416 | tf_op jit(solution)/shard_map/ppermute | solution.py:21
  170.8 3.3 %collective-permute-start.31 = (f32[18,1,256]{2,0,1:T(8,128)S(1)}, f32[18,1,256]{2,0,1:T(8,128)S(1)}, u32[]{:S(2)}, u32[]{:S(2)}) collective-permute-start(f32[18,1,256]{2,0,1:T(8,128)S(1)} %get-tuple-element.15), channel_id=1, source_target_pairs={{0,1},{1,2},{2,3},{4,5},{5,6},{6,7},{8,9},{9,10},{10,11},{12,13},{... | collective-permute-start | bytes 55304 | tf_op jit(solution)/shard_map/ppermute | solution.py:20
  (168 shorter events, 76.1 us)
Async XLA Ops:
  0.8 25.3 %collective-permute-start.5 = (f32[1,16,256]{2,0,1:T(1,128)S(1)}, f32[1,16,256]{2,0,1:T(1,128)S(1)}, u32[]{:S(2)}, u32[]{:S(2)}) collective-permute-start(f32[1,16,256]{2,0,1:T(1,128)S(1)} %copy.63), channel_id=1, source_target_pairs={{4,0},{8,4},{12,8},{5,1},{9,5},{13,9},{6,2},{10,6},{14,10},{7,3},{... | collective-permute-start | bytes 49160 | tf_op jit(solution)/shard_map/ppermute | solution.py:21
  2.1 24.0 %collective-permute-start.4 = (f32[1,16,256]{2,0,1:T(1,128)S(1)}, f32[1,16,256]{2,0,1:T(1,128)S(1)}, u32[]{:S(2)}, u32[]{:S(2)}) collective-permute-start(f32[1,16,256]{2,0,1:T(1,128)S(1)} %copy.61), channel_id=1, source_target_pairs={{0,4},{4,8},{8,12},{1,5},{5,9},{9,13},{2,6},{6,10},{10,14},{3,7},{... | collective-permute-start | bytes 49160 | tf_op jit(solution)/shard_map/ppermute | solution.py:20
  8.5 15.0 %collective-permute-start.1 = (f32[1,16,256]{2,0,1:T(1,128)S(1)}, f32[1,16,256]{2,0,1:T(1,128)S(1)}, u32[]{:S(2)}, u32[]{:S(2)}) collective-permute-start(f32[1,16,256]{2,0,1:T(1,128)S(1)} %copy.57), channel_id=1, source_target_pairs={{4,0},{8,4},{12,8},{5,1},{9,5},{13,9},{6,2},{10,6},{14,10},{7,3},{... | collective-permute-start | bytes 49160 | tf_op jit(solution)/shard_map/ppermute | solution.py:21
  9.8 13.7 %collective-permute-start = (f32[1,16,256]{2,0,1:T(1,128)S(1)}, f32[1,16,256]{2,0,1:T(1,128)S(1)}, u32[]{:S(2)}, u32[]{:S(2)}) collective-permute-start(f32[1,16,256]{2,0,1:T(1,128)S(1)} %copy.56), channel_id=1, source_target_pairs={{0,4},{4,8},{8,12},{1,5},{5,9},{9,13},{2,6},{6,10},{10,14},{3,7},{... | collective-permute-start | bytes 49160 | tf_op jit(solution)/shard_map/ppermute | solution.py:20
  23.5 9.1 %collective-permute-start.2 = (f32[18,1,256]{2,0,1:T(8,128)S(1)}, f32[18,1,256]{2,0,1:T(8,128)S(1)}, u32[]{:S(2)}, u32[]{:S(2)}) collective-permute-start(f32[18,1,256]{2,0,1:T(8,128)S(1)} %get-tuple-element.23), channel_id=1, source_target_pairs={{0,1},{1,2},{2,3},{4,5},{5,6},{6,7},{8,9},{9,10},{10,11},{12,13},{... | collective-permute-start | bytes 55304 | tf_op jit(solution)/shard_map/ppermute | solution.py:20
  24.8 7.9 %collective-permute-start.3 = (f32[18,1,256]{2,0,1:T(8,128)S(1)}, f32[18,1,256]{2,0,1:T(8,128)S(1)}, u32[]{:S(2)}, u32[]{:S(2)}) collective-permute-start(f32[18,1,256]{2,0,1:T(8,128)S(1)} %get-tuple-element.24), channel_id=1, source_target_pairs={{1,0},{2,1},{3,2},{5,4},{6,5},{7,6},{9,8},{10,9},{11,10},{13,12},{... | collective-permute-start | bytes 55304 | tf_op jit(solution)/shard_map/ppermute | solution.py:21
  26.1 7.3 %collective-permute-start.6 = (f32[18,1,256]{2,0,1:T(8,128)S(1)}, f32[18,1,256]{2,0,1:T(8,128)S(1)}, u32[]{:S(2)}, u32[]{:S(2)}) collective-permute-start(f32[18,1,256]{2,0,1:T(8,128)S(1)} %get-tuple-element.25), channel_id=1, source_target_pairs={{0,1},{1,2},{2,3},{4,5},{5,6},{6,7},{8,9},{9,10},{10,11},{12,13},{... | collective-permute-start | bytes 55304 | tf_op jit(solution)/shard_map/ppermute | solution.py:20
  37.3 5.4 %collective-permute-start.8 = (f32[1,16,256]{2,0,1:T(1,128)S(1)}, f32[1,16,256]{2,0,1:T(1,128)S(1)}, u32[]{:S(2)}, u32[]{:S(2)}) collective-permute-start(f32[1,16,256]{2,0,1:T(1,128)S(1)} %get-tuple-element.41), channel_id=1, source_target_pairs={{0,4},{4,8},{8,12},{1,5},{5,9},{9,13},{2,6},{6,10},{10,14},{3,7},{... | collective-permute-start | bytes 49160 | tf_op jit(solution)/shard_map/ppermute | solution.py:20
  40.8 5.6 %collective-permute-start.9 = (f32[1,16,256]{2,0,1:T(1,128)S(1)}, f32[1,16,256]{2,0,1:T(1,128)S(1)}, u32[]{:S(2)}, u32[]{:S(2)}) collective-permute-start(f32[1,16,256]{2,0,1:T(1,128)S(1)} %get-tuple-element.42), channel_id=1, source_target_pairs={{4,0},{8,4},{12,8},{5,1},{9,5},{13,9},{6,2},{10,6},{14,10},{7,3},{... | collective-permute-start | bytes 49160 | tf_op jit(solution)/shard_map/ppermute | solution.py:21
  47.1 9.8 %collective-permute-start.10 = (f32[18,1,256]{2,0,1:T(8,128)}, f32[18,1,256]{2,0,1:T(8,128)S(1)}, u32[]{:S(2)}, u32[]{:S(2)}) collective-permute-start(f32[18,1,256]{2,0,1:T(8,128)} %get-tuple-element.21), channel_id=1, source_target_pairs={{0,1},{1,2},{2,3},{4,5},{5,6},{6,7},{8,9},{9,10},{10,11},{12,13},{... | collective-permute-start | bytes 55304 | tf_op jit(solution)/shard_map/ppermute | solution.py:20
  50.1 6.8 %collective-permute-start.11 = (f32[18,1,256]{2,0,1:T(8,128)}, f32[18,1,256]{2,0,1:T(8,128)}, u32[]{:S(2)}, u32[]{:S(2)}) collective-permute-start(f32[18,1,256]{2,0,1:T(8,128)} %get-tuple-element.22), channel_id=1, source_target_pairs={{1,0},{2,1},{3,2},{5,4},{6,5},{7,6},{9,8},{10,9},{11,10},{13,12},{... | collective-permute-start | bytes 55304 | tf_op jit(solution)/shard_map/ppermute | solution.py:21
  58.6 16.3 %collective-permute-start.12 = (f32[1,16,256]{2,0,1:T(1,128)S(1)}, f32[1,16,256]{2,0,1:T(1,128)S(1)}, u32[]{:S(2)}, u32[]{:S(2)}) collective-permute-start(f32[1,16,256]{2,0,1:T(1,128)S(1)} %get-tuple-element.37), channel_id=1, source_target_pairs={{0,4},{4,8},{8,12},{1,5},{5,9},{9,13},{2,6},{6,10},{10,14},{3,7},{... | collective-permute-start | bytes 49160 | tf_op jit(solution)/shard_map/ppermute | solution.py:20
  62.2 12.7 %collective-permute-start.13 = (f32[1,16,256]{2,0,1:T(1,128)S(1)}, f32[1,16,256]{2,0,1:T(1,128)S(1)}, u32[]{:S(2)}, u32[]{:S(2)}) collective-permute-start(f32[1,16,256]{2,0,1:T(1,128)S(1)} %get-tuple-element.38), channel_id=1, source_target_pairs={{4,0},{8,4},{12,8},{5,1},{9,5},{13,9},{6,2},{10,6},{14,10},{7,3},{... | collective-permute-start | bytes 49160 | tf_op jit(solution)/shard_map/ppermute | solution.py:21
  74.9 5.3 %collective-permute-start.14 = (f32[18,1,256]{2,0,1:T(8,128)S(1)}, f32[18,1,256]{2,0,1:T(8,128)S(1)}, u32[]{:S(2)}, u32[]{:S(2)}) collective-permute-start(f32[18,1,256]{2,0,1:T(8,128)S(1)} %get-tuple-element.19), channel_id=1, source_target_pairs={{0,1},{1,2},{2,3},{4,5},{5,6},{6,7},{8,9},{9,10},{10,11},{12,13},{... | collective-permute-start | bytes 55304 | tf_op jit(solution)/shard_map/ppermute | solution.py:20
  89.7 6.3 %collective-permute-start.16 = (f32[5,8,128]{2,1,0:T(8,128)S(1)}, f32[5,8,128]{2,1,0:T(8,128)S(1)}, u32[]{:S(2)}, u32[]{:S(2)}) collective-permute-start(f32[5,8,128]{2,1,0:T(8,128)S(1)} %bitcast.195), channel_id=1, source_target_pairs={{4,0},{8,4},{12,8},{5,1},{9,5},{13,9},{6,2},{10,6},{14,10},{7,3},{... | collective-permute-start | bytes 61448 | tf_op jit(solution)/shard_map/ppermute | solution.py:29
  96.3 6.5 %collective-permute-start.18 = (f32[5,4,8,128]{3,1,2,0:T(4,128)S(1)}, f32[5,4,8,128]{3,1,2,0:T(4,128)S(1)}, u32[]{:S(2)}, u32[]{:S(2)}) collective-permute-start(f32[5,4,8,128]{3,1,2,0:T(4,128)S(1)} %get-tuple-element.14), channel_id=1, source_target_pairs={{4,0},{8,4},{12,8},{5,1},{9,5},{13,9},{6,2},{10,6},{14,10},{7,3},{... | collective-permute-start | bytes 245768 | tf_op jit(solution)/shard_map/ppermute | solution.py:21
  97.6 7.0 %collective-permute-start.17 = (f32[5,4,8,128]{3,1,2,0:T(4,128)S(1)}, f32[5,4,8,128]{3,1,2,0:T(4,128)S(1)}, u32[]{:S(2)}, u32[]{:S(2)}) collective-permute-start(f32[5,4,8,128]{3,1,2,0:T(4,128)S(1)} %get-tuple-element.13), channel_id=1, source_target_pairs={{0,4},{4,8},{8,12},{1,5},{5,9},{9,13},{2,6},{6,10},{10,14},{3,7},{... | collective-permute-start | bytes 245768 | tf_op jit(solution)/shard_map/ppermute | solution.py:20
  121.4 6.2 %collective-permute-start.22 = (f32[1,1,8,128]{3,1,2,0:T(1,128)S(1)}, f32[1,1,8,128]{3,1,2,0:T(1,128)S(1)}, u32[]{:S(2)}, u32[]{:S(2)}) collective-permute-start(f32[1,1,8,128]{3,1,2,0:T(1,128)S(1)} %slice.726), channel_id=1, source_target_pairs={{4,0},{8,4},{12,8},{5,1},{9,5},{13,9},{6,2},{10,6},{14,10},{7,3},{... | collective-permute-start | bytes 12296 | tf_op jit(solution)/shard_map/ppermute | solution.py:21
  122.7 6.2 %collective-permute-start.21 = (f32[1,1,8,128]{3,1,2,0:T(1,128)S(1)}, f32[1,1,8,128]{3,1,2,0:T(1,128)S(1)}, u32[]{:S(2)}, u32[]{:S(2)}) collective-permute-start(f32[1,1,8,128]{3,1,2,0:T(1,128)S(1)} %dynamic-slice_bitcast_fusion), channel_id=1, source_target_pairs={{0,4},{4,8},{8,12},{1,5},{5,9},{9,13},{2,6},{6,10},{10,14},{3,7},{... | collective-permute-start | bytes 12296 | tf_op jit(solution)/shard_map/ppermute | solution.py:20
  129.0 7.7 %collective-permute-start.23 = (f32[1,19,1,128]{3,1,2,0:T(8,128)S(1)}, f32[1,19,1,128]{3,1,2,0:T(8,128)S(1)}, u32[]{:S(2)}, u32[]{:S(2)}) collective-permute-start(f32[1,19,1,128]{3,1,2,0:T(8,128)S(1)} %get-tuple-element.55), channel_id=1, source_target_pairs={{0,1},{1,2},{2,3},{4,5},{5,6},{6,7},{8,9},{9,10},{10,11},{12,13},{... | collective-permute-start | bytes 29192 | tf_op jit(solution)/shard_map/ppermute | solution.py:20
  143.7 5.6 %collective-permute-start.25 = (f32[1,16,256]{2,0,1:T(1,128)S(1)}, f32[1,16,256]{2,0,1:T(1,128)S(1)}, u32[]{:S(2)}, u32[]{:S(2)}) collective-permute-start(f32[1,16,256]{2,0,1:T(1,128)S(1)} %get-tuple-element.33), channel_id=1, source_target_pairs={{0,4},{4,8},{8,12},{1,5},{5,9},{9,13},{2,6},{6,10},{10,14},{3,7},{... | collective-permute-start | bytes 49160 | tf_op jit(solution)/shard_map/ppermute | solution.py:20
  147.9 5.6 %collective-permute-start.26 = (f32[1,16,256]{2,0,1:T(1,128)S(1)}, f32[1,16,256]{2,0,1:T(1,128)S(1)}, u32[]{:S(2)}, u32[]{:S(2)}) collective-permute-start(f32[1,16,256]{2,0,1:T(1,128)S(1)} %get-tuple-element.34), channel_id=1, source_target_pairs={{4,0},{8,4},{12,8},{5,1},{9,5},{13,9},{6,2},{10,6},{14,10},{7,3},{... | collective-permute-start | bytes 49160 | tf_op jit(solution)/shard_map/ppermute | solution.py:21
  161.2 5.4 %collective-permute-start.29 = (f32[1,16,256]{2,0,1:T(1,128)S(1)}, f32[1,16,256]{2,0,1:T(1,128)S(1)}, u32[]{:S(2)}, u32[]{:S(2)}) collective-permute-start(f32[1,16,256]{2,0,1:T(1,128)S(1)} %get-tuple-element.29), channel_id=1, source_target_pairs={{0,4},{4,8},{8,12},{1,5},{5,9},{9,13},{2,6},{6,10},{10,14},{3,7},{... | collective-permute-start | bytes 49160 | tf_op jit(solution)/shard_map/ppermute | solution.py:20
  165.1 5.6 %collective-permute-start.30 = (f32[1,16,256]{2,0,1:T(1,128)S(1)}, f32[1,16,256]{2,0,1:T(1,128)S(1)}, u32[]{:S(2)}, u32[]{:S(2)}) collective-permute-start(f32[1,16,256]{2,0,1:T(1,128)S(1)} %get-tuple-element.30), channel_id=1, source_target_pairs={{4,0},{8,4},{12,8},{5,1},{9,5},{13,9},{6,2},{10,6},{14,10},{7,3},{... | collective-permute-start | bytes 49160 | tf_op jit(solution)/shard_map/ppermute | solution.py:21
  (16 other events, 76.0 us)
where the time goes:
time: 183 us; the launch traced here: 179 us
  starting transfers between devices  85.4 us (47%)
  waiting for transfers between devices  36.4 us (20%)
  local copies, waits for them, and re-layouts  31.6 us (17%)
  other arithmetic  21.6 us (12%)
  between operations  3.56 us (2%)
    ppermute x16, starting transfers between devices, padded(): before = lax.ppermute(last, axis, up)  63.3 us
    ppermute x16, waiting for transfers between devices, padded(): after = lax.ppermute(leading, axis, down)  27.9 us
    ppermute x16, starting transfers between devices, padded(): after = lax.ppermute(leading, axis, down)  20.9 us
    reduce_sum x3, other arithmetic, pair_sum(): return block_in.reshape(width_x, half_y, 2, half_z, 2).sum(axis=(2, 4))  10.4 us
    ppermute x1, waiting for transfers between devices, passed_along(): return lax.ppermute(array, axis, pairs)  4.99 us
    dynamic_update_slice x2, local copies, waits for them, and re-layouts, coarse_extend(): lax.dynamic_update_slice_in_dim(base_block, ahead_planes, rim_width + cou...  4.83 us
    slice x1, local copies, waits for them, and re-layouts, body(): face_above[:, :, 1::2].reshape(width_x, half_y, 2, half_z).sum(axis=2)  4.49 us
    add x4, other arithmetic, smooth(): field_in = center + OMEGA * (source - product) / faces_zero[7]  3.66 us
  transfers between devices with their start and end apart: 33, of which 16 were waited for; matrix products, arithmetic and copies ran while one was open for 14% of the time, Pallas kernels for 0%

commit v1 on v0

v1 whole, which is shorter than its diff:
```python
import functools
import jax
import jax.numpy as jnp
from jax import lax
from jax.experimental import pallas as pl
from jax.experimental.pallas import tpu as pltpu
from jax.sharding import PartitionSpec as P

OMEGA = 0.8
MESH = pl.DeviceIdType.MESH
HIGH = lax.Precision.HIGHEST

DIRS = [(dx, dy) for dx in (1, 0, -1) for dy in (1, 0, -1) if (dx, dy) != (0, 0)]
FROM = {0: 0, 1: 1, -1: 2}


def dot(a, b):
    return jnp.dot(a, b, precision=HIGH, preferred_element_type=jnp.float32)


def kernel(
    agg, k_in, s_in, p_in, out,
    ke, se, pe, khalo, shalo, phalo, fx, fy, fz, dg, wt, p1, p2, rr, rhalo,
    fields, cm, cl, cr, cs, ext, corr, local_sem, send_sem, recv_sem,
):
    f32 = jnp.float32
    width = 16
    slab, slabs = lax.axis_index("slab"), lax.axis_size("slab")
    subs = lax.axis_size("sub")
    rows = lax.axis_size("pencil") * subs
    row = lax.axis_index("pencil") * subs + lax.axis_index("sub")

    loads = [
        pltpu.make_async_copy(src, dst.at[3:19, 0:16], local_sem.at[i])
        for i, (src, dst) in enumerate(((k_in, ke), (p_in, pe), (s_in, se)))
    ]
    for load in loads:
        load.start()

    def exists(dx, dy):
        ok = None
        for pos, step, count in ((slab, dx, slabs), (row, dy, rows)):
            if step:
                here = (pos + step < count) if step > 0 else (pos > 0)
                ok = here if ok is None else jnp.logical_and(ok, here)
        return ok

    def device(dx, dy):
        r = row + dy
        return {"slab": slab + dx, "pencil": r // subs, "sub": r % subs}

    barrier = pltpu.get_barrier_semaphore()
    for dx, dy in DIRS:
        @pl.when(exists(dx, dy))
        def _():
            pl.semaphore_signal(barrier, inc=1, device_id=device(dx, dy), device_id_type=MESH)
    near_x = 1 + (slab > 0).astype(jnp.int32) + (slab < slabs - 1).astype(jnp.int32)
    near_y = 1 + (row > 0).astype(jnp.int32) + (row < rows - 1).astype(jnp.int32)

    def message(kind, d, src, dst):
        return pltpu.make_async_remote_copy(
            src_ref=src, dst_ref=dst,
            send_sem=send_sem.at[kind * 8 + d], recv_sem=recv_sem.at[kind * 8 + d],
            device_id=device(*DIRS[d]), device_id_type=MESH,
        )

    def fine_message(kind, d, body, halo, wide, corner):
        dx, dy = DIRS[d]
        if dy == 0:
            src0 = 19 - wide if dx > 0 else 3
            dst0 = 3 - wide if dx > 0 else 19
            return message(kind, d, body.at[src0:src0 + wide, 0:16], body.at[dst0:dst0 + wide, 0:16])
        src_row = 8 if dy > 0 else 0
        if dx == 0:
            src0, dst0, length = 3, 3, 16
        else:
            src0 = 19 - corner if dx > 0 else 3
            dst0 = 3 - corner if dx > 0 else 19
            length = corner
        return message(
            kind, d, body.at[src0:src0 + length, src_row:src_row + 8],
            halo.at[FROM[dy] - 1, dst0:dst0 + length],
        )

    def coarse_message(kind, d, q0, q1):
        dx, dy = DIRS[d]
        here = FROM[dy]
        qs = pl.ds(q0, q1 - q0)
        if dx > 0:
            return message(kind, d, cs.at[qs], cl.at[here, qs])
        if dx < 0:
            return message(kind, d, cm.at[0, qs, 0:32], cr.at[here, qs])
        return message(kind, d, cm.at[0, qs], cm.at[here, qs])

    kinds = {
        "k": lambda d: fine_message(0, d, ke, khalo, 3, 2),
        "p": lambda d: fine_message(1, d, pe, phalo, 3, 2),
        "s": lambda d: fine_message(2, d, se, shalo, 2, 1),
        "coef": lambda d: coarse_message(3, d, 1, 5),
        "rhs": lambda d: coarse_message(4, d, 0, 1),
        "post": lambda d: fine_message(5, d, rr, rhalo, 1, 0),
    }

    def each(name):
        return [d for d in range(8) if name != "post" or 0 in DIRS[d]]

    def send(name):
        for d in each(name):
            @pl.when(exists(*DIRS[d]))
            def _():
                kinds[name](d).start()

    def receive(name):
        for d in each(name):
            dx, dy = DIRS[d]
            @pl.when(exists(-dx, -dy))
            def _():
                kinds[name](d).wait_recv()

    def sent(name):
        for d in each(name):
            @pl.when(exists(*DIRS[d]))
            def _():
                kinds[name](d).wait_send()

    for load in loads:
        load.wait()
    pl.semaphore_wait(barrier, near_x * near_y - 1)
    send("k")
    send("p")
    send("s")

    def clear(ref, *index):
        view = ref.at[index]
        view[...] = jnp.zeros(view.shape, f32)

    for ref, halo, wide, corner in ((ke, khalo, 3, 2), (pe, phalo, 3, 2), (se, shalo, 2, 1)):
        for at in (slice(0, 3 - corner), slice(19 + corner, 22)):
            clear(halo, slice(0, 2), at)
        if wide < 3:
            clear(ref, slice(0, 1))
            clear(ref, slice(21, 22))
    for dx, dy in DIRS:
        @pl.when(jnp.logical_not(exists(-dx, -dy)))
        def _():
            for ref, halo, wide, corner in (
                (ke, khalo, 3, 2), (pe, phalo, 3, 2), (se, shalo, 2, 1), (rr, rhalo, 1, 0),
            ):
                if dy == 0:
                    at = slice(3 - wide, 3) if dx > 0 else slice(19, 19 + wide)
                    clear(ref, at, slice(0, 16))
                else:
                    lo, hi = {0: (3, 19), 1: (3 - corner, 3), -1: (19, 19 + corner)}[dx]
                    if hi > lo:
                        clear(halo, FROM[dy] - 1, slice(lo, hi))
            part = {0: cm, 1: cl, -1: cr}[dx]
            clear(part, FROM[dy])

    low_half = lax.broadcasted_iota(jnp.int32, (8, 256), 0) < 4
    y_at = lax.broadcasted_iota(jnp.int32, (24, 256), 0)
    z_at = lax.broadcasted_iota(jnp.int32, (24, 256), 1)
    y_rel = jnp.where(y_at < 20, y_at, y_at - 24)
    y_glob = y_rel + row * width
    ends_yz = (
        (y_glob == 0).astype(f32) + (y_glob == rows * width - 1).astype(f32)
        + (z_at == 0).astype(f32) + (z_at == 255).astype(f32)
    )
    odd_y = (y_at & 1) == 1
    odd_z = (z_at & 1) == 1

    def loop(lo, hi, step, unroll=2):
        def run(i, carry):
            step(i)
            return carry
        lax.fori_loop(lo, hi, run, 0, unroll=unroll)

    def set_rim(body, halo, lo, hi):
        def step(i):
            body[i, 16:24] = jnp.where(low_half, halo[1, i], halo[0, i])
        loop(lo, hi, step)

    def next_y(v):
        return pltpu.roll(v, 23, 0)

    def prev_y(v):
        return pltpu.roll(v, 1, 0)

    def next_z(v):
        return pltpu.roll(v, 255, 1)

    def prev_z(v):
        return pltpu.roll(v, 1, 1)

    def face(a, b):
        total = a + b
        return 2.0 * a * b / jnp.where(total > 0, total, 1.0)

    ids = [agg[slab * width + x] for x in range(width)]
    slots = [i - ids[0] for i in ids]
    live = slots[15]
    col = lax.broadcasted_iota(jnp.int32, (1, 256), 1)
    slot_col = jnp.zeros((1, 256), jnp.int32)
    cross_col = jnp.zeros((1, 256), jnp.int32)
    for x in range(width):
        inside = (col >> 4) == x
        slot_col = jnp.where(inside, slots[x], slot_col)
        if x < 15:
            cross_col = jnp.where(inside, (ids[x] != ids[x + 1]).astype(jnp.int32), cross_col)
    r168 = lax.broadcasted_iota(jnp.int32, (168, 256), 0)
    c168 = lax.broadcasted_iota(jnp.int32, (168, 256), 1)
    want = jnp.where(r168 < 128, r168 >> 3, (r168 >> 3) - 20 + live)
    gather = ((want == slot_col) & ((r168 & 7) == ((c168 & 15) >> 1))).astype(f32)
    gather_east = gather * cross_col.astype(f32)
    zr = lax.broadcasted_iota(jnp.int32, (256, 128), 0)
    zc = lax.broadcasted_iota(jnp.int32, (256, 128), 1)
    pair_z = ((zr >> 1) == zc).astype(f32)

    def coarsen(q, field, how):
        sums = dot(dot(how, field), pair_z)
        cm[0, q] = sums[0:128]
        cs[q] = sums[128:168]

    receive("k")
    set_rim(ke, khalo, 0, 22)

    def x_faces(i):
        fx[i] = face(ke[i], ke[i + 1])
    loop(0, 21, x_faces)

    def other_faces(i):
        k = ke[i]
        north = face(k, next_y(k))
        above = jnp.where(z_at == 255, 0.0, face(k, next_z(k)))
        south, below = prev_y(north), prev_z(above)
        x_glob = slab * width + i - 3
        ends_x = (x_glob == 0).astype(f32) + (x_glob == slabs * width - 1).astype(f32)
        bound = 2.0 * k * (ends_yz + ends_x)
        fy[i] = north
        fz[i] = above
        diag = fx[i - 1] + fx[i] + north + south + above + below + bound
        dg[i] = diag
        wt[i] = OMEGA / jnp.where(diag > 0, diag, 1.0)
        return north, above, south, below, bound

    def plain_faces(i):
        other_faces(i)

    def own_faces(i):
        north, above, south, below, bound = other_faces(i)
        fields[1, i - 3] = fx[i, 0:16]
        fields[2, i - 3] = jnp.where(odd_y, north, 0.0)[0:16]
        fields[3, i - 3] = jnp.where(odd_z, above, 0.0)[0:16]
        whole = bound + jnp.where(odd_y, north, south) + jnp.where(odd_z, above, below)
        fields[4, i - 3] = whole[0:16]

    loop(3, 19, own_faces)
    for q in range(1, 5):
        coarsen(q, fields[q].reshape(256, 256), gather_east if q == 1 else gather)
    send("coef")
    loop(1, 3, plain_faces)
    loop(19, 21, plain_faces)

    def beside(src, i):
        v = src[i]
        north, above = fy[i], fz[i]
        around = fx[i - 1] * src[i - 1] + fx[i] * src[i + 1]
        around = around + (north * next_y(v) + prev_y(north * v))
        return v, around + (above * next_z(v) + prev_z(above * v))

    def sweep(src, dst, lo, hi):
        def step(i):
            v, around = beside(src, i)
            dst[i] = (1.0 - OMEGA) * v + wt[i] * (se[i] + around)
        loop(lo, hi, step)

    receive("p")
    set_rim(pe, phalo, 0, 22)
    receive("s")
    set_rim(se, shalo, 1, 21)
    sweep(pe, p1, 1, 21)
    sweep(p1, p2, 2, 20)

    def residual(i):
        v, around = beside(p2, i)
        fields[0, i - 3] = (se[i] - dg[i] * v + around)[0:16]
    loop(3, 19, residual)
    coarsen(0, fields[0].reshape(256, 256), gather)
    send("rhs")

    rp = lax.broadcasted_iota(jnp.int32, (384, 64), 0)
    cp = lax.broadcasted_iota(jnp.int32, (384, 64), 1)
    place = (((rp >> 4) - (cp >> 4) == 4 + live) & ((rp & 15) == (cp & 15))).astype(f32)
    low_coarse = lax.broadcasted_iota(jnp.int32, (1, 8, 128), 1) < 4

    def joined(part, q, count):
        own = part[0, q].reshape(count, 8, 128)
        below = part[1, q].reshape(count, 8, 128)
        above = part[2, q].reshape(count, 8, 128)
        return jnp.concatenate([own, jnp.where(low_coarse, above, below)], axis=1)

    def extend(q):
        after = dot(place, joined(cr, q, 4).reshape(64, 128)).reshape(24, 16, 128)
        ext[q] = after
        ext[q, 0:5] += joined(cl, q, 5)
        ext[q, 4:20] += joined(cm, q, 16)

    receive("coef")
    for q in range(1, 5):
        extend(q)
    zl = lax.broadcasted_iota(jnp.int32, (16, 128), 1)
    def diagonal(t):
        diag = ext[4, t] + ext[1, t] + ext[1, t - 1]
        corr[2, t] = OMEGA / jnp.where(diag > 0, diag, 1.0)
    loop(1, 23, diagonal)
    receive("rhs")
    extend(0)

    def first(t):
        corr[0, t] = corr[2, t] * ext[0, t]
    loop(1, 23, first)
    for number, (lo, hi) in enumerate(((2, 22), (3, 21), (4, 20))):
        src, dst = number % 2, (number + 1) % 2
        def coarse_sweep(t):
            v = corr[src, t]
            north, above = ext[2, t], ext[3, t]
            around = ext[1, t] * corr[src, t + 1] + ext[1, t - 1] * corr[src, t - 1]
            around = around + (north * pltpu.roll(v, 15, 0) + pltpu.roll(north * v, 1, 0))
            around = around + (above * pltpu.roll(v, 127, 1) + pltpu.roll(above * v, 1, 1))
            corr[dst, t] = (1.0 - OMEGA) * v + corr[2, t] * (ext[0, t] + around)
        loop(lo, hi, coarse_sweep)

    ru = lax.broadcasted_iota(jnp.int32, (24, 256), 0)
    cu = lax.broadcasted_iota(jnp.int32, (24, 256), 1)
    same_y = (cu & 15) == jnp.where(ru < 20, ru >> 1, (ru >> 1) + 4)
    spread = jnp.concatenate(
        [(same_y & ((cu >> 4) == slots[x])).astype(f32) for x in range(width)], axis=0
    )
    er = lax.broadcasted_iota(jnp.int32, (128, 256), 0)
    ec = lax.broadcasted_iota(jnp.int32, (128, 256), 1)
    twice_z = ((ec >> 1) == er).astype(f32)
    fine = dot(dot(spread, corr[1, 4:20].reshape(256, 128)), twice_z).reshape(16, 24, 256)
    p1[3:19] = p2[3:19] + fine
    p1[2] = p2[2] + fine[0]
    p1[19] = p2[19] + fine[15]
    sweep(p1, rr, 3, 19)
    send("post")
    receive("post")
    set_rim(rr, rhalo, 3, 19)

    def last(i):
        v, around = beside(rr, i)
        out[i - 3] = ((1.0 - OMEGA) * v + wt[i] * (se[i] + around))[0:16]
    loop(3, 19, last)
    for name in kinds:
        sent(name)


def body(permeability, source, pressure, aggregate):
    f32 = jnp.float32
    shape = permeability.shape
    block = pltpu.VMEM((22, 24, 256), f32)
    halo = pltpu.VMEM((2, 22, 8, 256), f32)
    hbm = pl.BlockSpec(memory_space=pl.ANY)
    return pl.pallas_call(
        kernel,
        out_shape=jax.ShapeDtypeStruct(shape, f32),
        in_specs=[pl.BlockSpec(memory_space=pltpu.SMEM), hbm, hbm, hbm],
        out_specs=pl.BlockSpec(memory_space=pltpu.VMEM),
        scratch_shapes=[block, block, block, halo, halo, halo]
        + [block] * 8
        + [
            halo,
            pltpu.VMEM((5, 16, 16, 256), f32),
            pltpu.VMEM((3, 5, 128, 128), f32),
            pltpu.VMEM((3, 5, 40, 128), f32),
            pltpu.VMEM((3, 5, 32, 128), f32),
            pltpu.VMEM((5, 40, 128), f32),
            pltpu.VMEM((5, 24, 16, 128), f32),
            pltpu.VMEM((3, 24, 16, 128), f32),
            pltpu.SemaphoreType.DMA((3,)),
            pltpu.SemaphoreType.DMA((48,)),
            pltpu.SemaphoreType.DMA((48,)),
        ],
        compiler_params=pltpu.CompilerParams(
            collective_id=0, has_side_effects=True, vmem_limit_bytes=40 * 2**20
        ),
    )(aggregate, permeability, source, pressure)


def solution(mesh):
    spec = P(("real", "slab"), ("pencil", "sub"), None)
    return jax.shard_map(
        body, mesh=mesh, in_specs=(spec, spec, spec, P("real")), out_specs=spec, check_vma=False
    )
```

time: 183 us -> 34.1 us (0.19); the launches traced: 179 us -> 33.9 us
  starting transfers between devices: 85.4 us -> 0 us
  waiting for transfers between devices: 36.4 us -> 0 us
  Pallas kernels: 0 us -> 29.6 us
  local copies, waits for them, and re-layouts: 31.6 us -> 4.21 us
  other arithmetic: 21.6 us -> 0 us
  between operations: 3.56 us -> 0.01 us
    ppermute x33 -> x0, starting transfers between devices: 85.4 us -> none  [the longest x16 63.3 us: padded(): before = lax.ppermute(last, axis, up)]
    ppermute x33 -> x0, waiting for transfers between devices: 36.4 us -> none  [the longest x16 27.9 us: padded(): after = lax.ppermute(leading, axis, down)]
    pallas_call x0 -> x1, Pallas kernels: none -> 29.6 us  [body(): pl.pallas_call(kernel, out_shape=jax.ShapeDtypeStruct(shape, f32), in_spe...]
    slice x31 -> x0, local copies, waits for them, and re-layouts: 11.6 us -> none  [the longest x1 4.49 us: body(): face_above[:, :, 1::2].reshape(width_x, half_y, 2, half_z).sum(axis=2)]
    reduce_sum x5 -> x0, other arithmetic: 11.3 us -> none  [the longest x3 10.4 us: pair_sum(): return block_in.reshape(width_x, half_y, 2, half_z, 2).sum(axis=(2, 4))]
    dynamic_update_slice x2 -> x0, local copies, waits for them, and re-layouts: 4.83 us -> none  [coarse_extend(): lax.dynamic_update_slice_in_dim(base_block, ahead_planes, rim_width + cou...]
    add x14 -> x0, other arithmetic: 4.61 us -> none  [the longest x4 3.66 us: smooth(): field_in = center + OMEGA * (source - product) / faces_zero[7]]
    mul x2 -> x0, local copies, waits for them, and re-layouts: 3.94 us -> none  [the longest x1 1.99 us: body(): east_part = pair_sum(face_east * crossing[:, None, None])]
  transfers between devices with their start and end apart: 33 -> 0, of which waited for: 16 -> 0; matrix products, arithmetic and copies ran while one was open for 14% -> 0% of each run, Pallas kernels for 0% -> 0%
where the time goes in v1:
time: 34.1 us; the launch traced here: 33.9 us
  Pallas kernels  29.6 us (87%)
  local copies, waits for them, and re-layouts  4.21 us (12%)
    pallas_call x1, Pallas kernels, body(): pl.pallas_call(kernel, out_shape=jax.ShapeDtypeStruct(shape, f32), in_spe...  29.6 us
    unnamed x9, local copies, waits for them, and re-layouts  4.21 us

profile of v1, /device:TPU:0, one launch (start us, length us, event | category | flops | bytes accessed | tf_op | source)
XLA Modules:
  0.0 33.9 jit_solution(17950082616255487529)
XLA Ops:
  0.0 0.0 copy-start
  0.0 0.9 %copy-done = f32[16,16,256]{2,1,0:T(8,128)S(1)} copy-done((f32[16,16,256]{2,1,0:T(8,128)S(1)}, f32[16,16,256]{2,1,0:T(8,128)}, u32[]{:S(2)}) %copy-start) | copy-done | bytes 262168
  1.0 0.0 copy-start.1
  1.0 0.9 %copy-done.1 = f32[16,16,256]{2,1,0:T(8,128)S(1)} copy-done((f32[16,16,256]{2,1,0:T(8,128)S(1)}, f32[16,16,256]{2,1,0:T(8,128)}, u32[]{:S(2)}) %copy-start.1) | copy-done | bytes 262168
  1.9 0.0 copy-start.2
  1.9 0.9 %copy-done.2 = f32[16,16,256]{2,1,0:T(8,128)S(1)} copy-done((f32[16,16,256]{2,1,0:T(8,128)S(1)}, f32[16,16,256]{2,1,0:T(8,128)}, u32[]{:S(2)}) %copy-start.2) | copy-done | bytes 262168
  2.9 0.0 copy-start.3
  2.9 0.7 %copy-done.3 = s32[64]{0:T(128)S(1)} copy-done((s32[64]{0:T(128)S(1)}, s32[64]{0:T(128)}, u32[]{:S(2)}) %copy-start.3) | copy-done | bytes 280
  3.5 29.6 %shard_map.46 = f32[16,16,256]{2,1,0:T(8,128)S(1)} custom-call(s32[64]{0:T(128)S(1)} %copy-done.3, f32[16,16,256]{2,1,0:T(8,128)S(1)} %copy-done, f32[16,16,256]{2,1,0:T(8,128)S(1)} %copy-done.1, f32[16,16,256]{2,1,0:T(8,128)S(1)} %copy-done.2), custom_call_target="tpu_custom_call" | custom-call | tf_op jit(solution)/shard_map/pallas_call | solution.py:364
  33.2 0.7 %copy.6 = f32[16,16,256]{2,1,0:T(8,128)} copy(f32[16,16,256]{2,1,0:T(8,128)S(1)} %shard_map.46) | data formatting | bytes 524288
Async XLA Ops:
  0.0 0.9 %copy-start = (f32[16,16,256]{2,1,0:T(8,128)S(1)}, f32[16,16,256]{2,1,0:T(8,128)}, u32[]{:S(2)}) copy-start(f32[16,16,256]{2,1,0:T(8,128)} %k_in.1) | copy-start | bytes 786436
  1.0 0.9 %copy-start.1 = (f32[16,16,256]{2,1,0:T(8,128)S(1)}, f32[16,16,256]{2,1,0:T(8,128)}, u32[]{:S(2)}) copy-start(f32[16,16,256]{2,1,0:T(8,128)} %s_in.1) | copy-start | bytes 786436
  1.9 0.9 %copy-start.2 = (f32[16,16,256]{2,1,0:T(8,128)S(1)}, f32[16,16,256]{2,1,0:T(8,128)}, u32[]{:S(2)}) copy-start(f32[16,16,256]{2,1,0:T(8,128)} %p_in.1) | copy-start | bytes 786436
  2.9 0.7 %copy-start.3 = (s32[64]{0:T(128)S(1)}, s32[64]{0:T(128)}, u32[]{:S(2)}) copy-start(s32[64]{0:T(128)} %agg.1) | copy-start | bytes 772
